TPU v7x, 128 devices: a whole 4x4x4 slice. The times are simulated.
128 devices in a mesh: seq: 32 (over z, y, core), tp: 4 (over x).
Axes of the slice: x: 4, y: 4, z: 4, core: 2. Of those that a mesh axis runs over, the one named last changes fastest.
Arguments:
- query_proj: bfloat16 [6144, 3072], P('seq', 'tp'), may hold values from -6 to 6
- key_proj: bfloat16 [6144, 3072], P('seq', 'tp'), may hold values from -6 to 6
- value_proj: bfloat16 [6144, 3072], P('seq', 'tp'), may hold values from -6 to 6
- attn_output: bfloat16 [6144, 3072], P('seq', 'tp')
- out_grad: bfloat16 [6144, 3072], P('seq', 'tp'), may hold values from -6 to 6
- log_norm: float32 [6144, 24], P('seq', 'tp')
- router_logit: float32 [6144], P('seq'), may hold values from -4 to 4
- keep_positions: int32 [6144], replicated, may hold values from -1 to 32767, as said below
Outputs:
- query_grad: bfloat16 [6144, 3072], P('seq', 'tp')
- key_grad: bfloat16 [6144, 3072], P('seq', 'tp')
- value_grad: bfloat16 [6144, 3072], P('seq', 'tp')
- router_grad: float32 [6144], P('seq')
Inputs may be any that keep to these rules, and one draw needn't show every extreme that they name: `keep_positions`: slots s*192 to (s+1)*192 - 1 hold the kept positions of tokens s*1024 to (s+1)*1024 - 1 in increasing order, followed by -1 in the unused slots. Exactly 4096 tokens are kept in all; some shard fills all 192 slots and some shard keeps only 64.
All inputs are finite; a program needn't handle non-finite values.
Results may differ from a plain program's by a relative error of at most 0.03.
Values may be sent and summed in bfloat16 or wider, within the bound.
A program may use at most 128 MiB of HBM per device.

v0:
```python
import jax
import jax.numpy as jnp
from jax import lax
from jax.sharding import PartitionSpec as P


def pick_block(total_rows):
    for size in (1024, 512):
        return size
    return total_rows


def body(
    query_proj, key_proj, value_proj, attn_output, out_grad, log_norm, router_logit, keep_positions
):
    slots = query_proj.shape[0]
    heads = log_norm.shape[1]
    feature_count = query_proj.shape[1]
    head_dim = feature_count // heads
    scale = head_dim ** (-0.5)
    shard = lax.axis_index("seq")
    my_positions = lax.dynamic_slice_in_dim(keep_positions, shard * slots, slots)
    my_valid = my_positions >= 0
    gate = jax.nn.sigmoid(router_logit)
    slope = gate * (1.0 - gate)
    grad_wide = out_grad.astype(jnp.float32)
    output_wide = attn_output.astype(jnp.float32)
    partial_dot = jnp.sum(grad_wide * output_wide, axis=1)
    total_dot = lax.psum(partial_dot, "tp")
    router_grad = jnp.where(my_valid, slope * total_dot, jnp.float32(0.0))
    dout = (gate[:, None] * grad_wide).astype(jnp.bfloat16)
    delta = jnp.sum(
        (dout.astype(jnp.float32) * output_wide).reshape(slots, heads, head_dim), axis=2
    )
    local_key = key_proj.reshape(slots, heads, head_dim)
    local_value = value_proj.reshape(slots, heads, head_dim)
    query_all, dout_all = (
        lax.all_gather(query_proj, "seq", axis=0, tiled=True),
        lax.all_gather(dout, "seq", axis=0, tiled=True),
    )
    norm_all, delta_all = (
        lax.all_gather(log_norm, "seq", axis=0, tiled=True),
        lax.all_gather(delta, "seq", axis=0, tiled=True),
    )
    total_rows = query_all.shape[0]
    block = pick_block(total_rows)
    steps_count = total_rows // block

    def step(carry, index):
        key_acc, value_acc = carry
        start = index * block
        query_part = lax.dynamic_slice_in_dim(query_all, start, block, 0).reshape(
            block, heads, head_dim
        )
        dout_part = lax.dynamic_slice_in_dim(dout_all, start, block, 0).reshape(
            block, heads, head_dim
        )
        norm_part = lax.dynamic_slice_in_dim(norm_all, start, block, 0)
        delta_part = lax.dynamic_slice_in_dim(delta_all, start, block, 0)
        position_part = lax.dynamic_slice_in_dim(keep_positions, start, block, 0)
        allowed = (
            (position_part >= 0)[:, None]
            & my_valid[None, :]
            & (my_positions[None, :] <= position_part[:, None])
        )
        scores = (
            jnp.einsum("qhd,khd->hqk", query_part, local_key, preferred_element_type=jnp.float32)
            * scale
        )
        prob = jnp.where(allowed[None], jnp.exp(scores - norm_part.T[:, :, None]), jnp.float32(0.0))
        prob_low = prob.astype(jnp.bfloat16)
        dprob = jnp.einsum(
            "qhd,khd->hqk", dout_part, local_value, preferred_element_type=jnp.float32
        )
        dscore = (prob * (dprob - delta_part.T[:, :, None]) * scale).astype(jnp.bfloat16)
        value_acc = value_acc + jnp.einsum(
            "hqk,qhd->khd", prob_low, dout_part, preferred_element_type=jnp.float32
        )
        key_acc = key_acc + jnp.einsum(
            "hqk,qhd->khd", dscore, query_part, preferred_element_type=jnp.float32
        )
        term = jnp.einsum(
            "hqk,khd->qhd", dscore, local_key, preferred_element_type=jnp.float32
        ).reshape(block, feature_count)
        return ((key_acc, value_acc), term)

    empty = jnp.zeros((slots, heads, head_dim), jnp.float32)
    (key_acc, value_acc), key_terms = lax.scan(
        step, (empty, empty), jnp.arange(steps_count, dtype=jnp.int32)
    )
    key_grad = key_acc.reshape(slots, feature_count).astype(jnp.bfloat16)
    value_grad = value_acc.reshape(slots, feature_count).astype(jnp.bfloat16)
    key_terms = key_terms.reshape(total_rows, feature_count)
    key_grad, value_grad, terms = (key_grad, value_grad, key_terms)
    query_grad = lax.psum_scatter(terms, "seq", scatter_dimension=0, tiled=True).astype(
        jnp.bfloat16
    )
    return (query_grad, key_grad, value_grad, router_grad)


def solution(mesh):
    placed = (
        P("seq", "tp"),
        P("seq", "tp"),
        P("seq", "tp"),
        P("seq", "tp"),
        P("seq", "tp"),
        P("seq", "tp"),
        P("seq"),
        P(),
    )
    return jax.shard_map(
        body,
        mesh=mesh,
        in_specs=placed,
        out_specs=(P("seq", "tp"), P("seq", "tp"), P("seq", "tp"), P("seq")),
        check_vma=False,
    )
```

profile of v0, /device:TPU:102, one launch (start us, length us, event | category | flops | bytes accessed | tf_op | source)
XLA Modules:
  0.0 390.7 jit_solution(14763089223786794841)
XLA Ops:
  8.0 1.2 fusion.17
  9.2 7.5 %psum.7 = f32[192]{0:T(256)S(1)} all-reduce(f32[192]{0:T(256)S(1)} %fusion.17), channel_id=1, replica_groups=mesh['seq'=32,'tp'=4] {'tp'}, use_global_device_ids=true, to_apply=%region_5.6 | all-reduce | flops 192 | bytes 1536 | tf_op jit(solution)/shard_map/psum | solution.py:29
  16.7 1.3 fusion.19
  18.0 1.9 convert_multiply_fusion.1
  20.0 24.7 %all-gather = f32[32,192,6]{1,2,0:T(8,128)S(1)} all-gather(f32[1,192,6]{1,2,0:T(8,128)} %bitcast.93), channel_id=1, replica_groups=mesh['seq'=32,'tp'=4] {'seq'}, dimensions={0}, use_global_device_ids=true | all-gather | bytes 152064 | tf_op jit(solution)/shard_map/all_gather | solution.py:42
  46.1 22.5 %all-gather.1 = f32[32,192,6]{1,2,0:T(8,128)S(1)} all-gather(f32[1,192,6]{1,2,0:T(8,128)S(1)} %copy.47), channel_id=1, replica_groups=mesh['seq'=32,'tp'=4] {'seq'}, dimensions={0}, use_global_device_ids=true | all-gather | bytes 152064 | tf_op jit(solution)/shard_map/all_gather | solution.py:43
  70.4 54.6 %all-gather.7.cloned.1.call-done = bf16[6144,768]{1,0:T(8,128)(2,1)} async-done(((bf16[192,768]{1,0:T(8,128)(2,1)}), bf16[6144,768]{1,0:T(8,128)(2,1)}) %all-gather.7.cloned.1.call-update) | async-done | bytes 9437200 | tf_op jit(solution)/shard_map/all_gather | solution.py:39
  125.0 136.0 %while.15 = (s32[]{:T(128)}, f32[192,6,128]{2,0,1:T(8,128)}, f32[192,6,128]{2,0,1:T(8,128)}, f32[6,1024,768]{2,1,0:T(8,128)}, s32[6]{0:T(128)S(1)}, /*index=5*/b...) while((s32[]{:T(128)}, f32[192,6,128]{2,0,1:T(8,128)}, ...), condition=%wide.region_2.3_spmd.clone, body=%wide.region_1.0_spmd.clone.sunk | while | flops 1524106240 | bytes 78732696 | solution.py:88
  128.6 3.2 constant_dynamic-slice_fusion.3
  131.8 1.7 copy.77
  133.6 1.6 copy.78
  135.2 1.9 fusion.58
  137.1 1.1 fusion.60
  138.3 1.9 multiply_convert_fusion.2
  141.2 2.3 fusion.61
  143.4 2.4 copy.79
  145.8 1.9 constant_dynamic-update-slice_fusion.2
  151.3 3.2 constant_dynamic-slice_fusion.3
  154.5 1.7 copy.77
  156.2 1.6 copy.78
  157.8 1.9 fusion.58
  159.8 1.1 fusion.60
  160.9 1.9 multiply_convert_fusion.2
  163.8 2.3 fusion.61
  166.1 2.4 copy.79
  168.4 1.9 constant_dynamic-update-slice_fusion.2
  174.0 3.2 constant_dynamic-slice_fusion.3
  177.2 1.7 copy.77
  178.9 1.6 copy.78
  180.5 1.9 fusion.58
  182.4 1.1 fusion.60
  183.6 1.9 multiply_convert_fusion.2
  186.5 2.3 fusion.61
  188.7 2.4 copy.79
  191.1 1.9 constant_dynamic-update-slice_fusion.2
  196.7 3.2 constant_dynamic-slice_fusion.3
  199.9 1.7 copy.77
  201.6 1.6 copy.78
  203.2 1.9 fusion.58
  205.1 1.1 fusion.60
  206.3 1.9 multiply_convert_fusion.2
  209.2 2.3 fusion.61
  211.4 2.4 copy.79
  213.8 1.9 constant_dynamic-update-slice_fusion.2
  219.3 3.2 constant_dynamic-slice_fusion.3
  222.5 1.7 copy.77
  224.2 1.6 copy.78
  225.9 1.9 fusion.58
  227.8 1.1 fusion.60
  229.0 1.9 multiply_convert_fusion.2
  231.8 2.3 fusion.61
  234.1 2.4 copy.79
  236.5 1.8 constant_dynamic-update-slice_fusion.2
  241.9 3.2 constant_dynamic-slice_fusion.3
  245.2 1.7 copy.77
  246.9 1.6 copy.78
  248.5 1.9 fusion.58
  250.4 1.1 fusion.60
  251.6 1.9 multiply_convert_fusion.2
  254.5 2.3 fusion.61
  256.7 2.4 copy.79
  259.1 1.9 constant_dynamic-update-slice_fusion.2
  263.5 118.8 %reduce-scatter.2.cloned.1.call-done = f32[192,768]{1,0:T(8,128)} async-done(((f32[6144,768]{1,0:T(8,128)}), f32[192,768]{1,0:T(8,128)}) %reduce-scatter.2.cloned.1.call-update) | async-done | bytes 589840 | tf_op jit(solution)/shard_map/reduce_scatter | solution.py:95
  382.3 1.8 convert_element_type.37
  (155 shorter events, 30.2 us)
Async XLA Ops:
  7.2 62.3 %copy-start = (bf16[192,768]{1,0:T(8,128)(2,1)S(1)}, bf16[192,768]{1,0:T(8,128)(2,1)}, u32[]{:S(2)}) copy-start(bf16[192,768]{1,0:T(8,128)(2,1)} %param.11) | copy-start | bytes 884740
  7.2 62.3 %copy-start.10 = (bf16[192,768]{1,0:T(8,128)(2,1)S(1)}, bf16[192,768]{1,0:T(8,128)(2,1)}, u32[]{:S(2)}) copy-start(bf16[192,768]{1,0:T(8,128)(2,1)} %param.12) | copy-start | bytes 884740
  7.2 63.2 %all-gather.5.cloned.1.call-start = ((), (), s32[]{:S(2)}) async-start(), calls=%async_computation.1 | async-start | bytes 9732096 | tf_op jit(solution)/shard_map/all_gather | solution.py:38
  7.9 117.1 %all-gather.7.cloned.1.call-start = ((), (), s32[]{:S(2)}) async-start(), calls=%async_computation.2 | async-start | bytes 9732096 | tf_op jit(solution)/shard_map/all_gather | solution.py:39
  20.0 362.4 %reduce-scatter.2.cloned.1.call-start = ((), (), s32[]{:S(2)}) async-start(), calls=%async_computation.3 | async-start | bytes 19464192 | tf_op jit(solution)/shard_map/reduce_scatter | solution.py:95
  135.2 1.9 copy-start.1
  135.2 1.9 copy-start.6
  135.2 1.9 copy-start.7
  137.1 1.1 copy-start.11
  138.2 1.9 copy-start.8
  138.3 1.9 copy-start.3
  140.2 1.0 copy-start.2
  141.2 2.3 copy-start.4
  157.8 1.9 copy-start.1
  157.8 1.9 copy-start.6
  157.8 1.9 copy-start.7
  159.7 1.1 copy-start.11
  160.9 1.9 copy-start.8
  160.9 1.9 copy-start.3
  162.8 1.0 copy-start.2
  163.8 2.3 copy-start.4
  180.5 1.9 copy-start.1
  180.5 1.9 copy-start.6
  180.5 1.9 copy-start.7
  182.4 1.1 copy-start.11
  183.6 1.9 copy-start.8
  183.6 1.9 copy-start.3
  185.5 1.0 copy-start.2
  186.5 2.3 copy-start.4
  203.2 1.9 copy-start.1
  203.2 1.9 copy-start.6
  203.2 1.9 copy-start.7
  205.1 1.1 copy-start.11
  206.3 1.9 copy-start.8
  206.3 1.9 copy-start.3
  208.2 1.0 copy-start.2
  209.2 2.3 copy-start.4
  225.9 1.9 copy-start.1
  225.9 1.9 copy-start.6
  225.9 1.9 copy-start.7
  227.8 1.1 copy-start.11
  228.9 1.9 copy-start.8
  228.9 1.9 copy-start.3
  230.9 1.0 copy-start.2
  231.8 2.3 copy-start.4
  248.5 1.9 copy-start.1
  248.5 1.9 copy-start.6
  248.5 1.9 copy-start.7
  250.4 1.1 copy-start.11
  251.6 1.9 copy-start.8
  251.6 1.9 copy-start.3
  253.5 1.0 copy-start.2
  254.5 2.3 copy-start.4
  261.0 1.1 copy-start.5
  261.0 1.8 copy-start.9
Sparse Core Ops, SparseCore 0:
  10.3 56.8 all-gather.4
  70.0 54.9 all-gather.6
  261.1 121.1 reduce-scatter.1
where the time goes:
time: 394 us; the launch traced here: 391 us
  waiting for transfers between devices  174 us (44%)
  local copies, waits for them, and re-layouts  77.7 us (20%)
  blocking collectives  54.7 us (14%)
  matrix products  47.9 us (12%)
  other arithmetic  17.6 us (4%)
  between operations  13.8 us (4%)
  loops' own time  4.71 us (1%)
    reduce_scatter x1, waiting for transfers between devices, body(): lax.psum_scatter(terms, 'seq', scatter_dimension=0, tiled=True)  119 us
    all_gather x1, waiting for transfers between devices, body(): lax.all_gather(dout, 'seq', axis=0, tiled=True)  54.6 us
    dynamic_slice x12, local copies, waits for them, and re-layouts, step(): lax.dynamic_slice_in_dim(dout_all, start, block, 0)  29 us
    dynamic_update_slice x12, local copies, waits for them, and re-layouts, body(): lax.scan(step, (empty, empty), jnp.arange(steps_count, dtype=jnp.int32))  25.5 us
    all_gather x1, blocking collectives, body(): lax.all_gather(log_norm, 'seq', axis=0, tiled=True)  24.7 us
    all_gather x1, blocking collectives, body(): lax.all_gather(delta, 'seq', axis=0, tiled=True)  22.5 us
    dot_general x6, matrix products, step(): jnp.einsum('hqk,khd->qhd', dscore, local_key, preferred_element_type=jnp....  13.5 us
    dot_general x6, matrix products, step(): jnp.einsum('qhd,khd->hqk', dout_part, local_value, preferred_element_type...  11.3 us
  transfers between devices with their start and end apart: 3, of which 2 were waited for; matrix products, arithmetic and copies ran while one was open for 2% of the time, Pallas kernels for 0%

commit v1 on v0

v1 whole, which is shorter than its diff:
```python
import math

import jax
import jax.numpy as jnp
from jax import lax
from jax.experimental import pallas as pl
from jax.experimental.pallas import tpu as pltpu
from jax.sharding import PartitionSpec as P

MESH = pl.DeviceIdType.MESH
LOG2E = math.log2(math.e)
SLOTS = 192
HEADS = 6
DIM = 128
SHARDS = 32
CUT = 10
REST = SHARDS - CUT
BLOCK = 4
FAR = 1e30
NEVER = 1e9


def column(row):
    top = jnp.broadcast_to(row[:, :128], (128, 128)).T
    rest = jnp.concatenate([row[:, 128:], row[:, 128:]], axis=1)
    low = jnp.broadcast_to(rest, (128, 128)).T
    return jnp.concatenate([top, low[:64]], axis=0)


def kernel(
    q_hbm, k_hbm, v_hbm, o_ref, g_ref, ln_ref, logit_ref, pos_ref,
    dq_out, dk_out, dv_out, rg_out,
    dout, stat, rbuf, kbuf, vbuf, qbuf, gbuf, sbuf, rowid, dkacc, dvacc, dqacc,
    dksend, dvsend, dqsend, dkrecv, dvrecv, dqrecv,
    kv_ssem, q_ssem, kv_rsem, q_rsem, dkv_ssem, dq_ssem, dkv_rsem, dq_rsem, r_ssem, r_rsem,
):
    me = lax.axis_index("seq")
    tp = lax.axis_index("tp")
    z, y, c = me // 8, (me // 2) % 4, me % 2

    barrier = pltpu.get_barrier_semaphore()

    def greet(i, _):
        pl.semaphore_signal(barrier, inc=1, device_id=((me + i) % SHARDS, tp), device_id_type=MESH)
        return 0

    lax.fori_loop(1, SHARDS, greet, 0)
    for i in range(1, 4):
        pl.semaphore_signal(barrier, inc=1, device_id=(me, (tp + i) % 4), device_id_type=MESH)

    logit = logit_ref[...]
    gate = 1.0 / (1.0 + jnp.exp(-logit))
    valid = pos_ref[pl.ds(me, 1), :] >= 0
    gate_col = column(gate)
    lane = lax.broadcasted_iota(jnp.int32, (SLOTS, DIM), 1)
    norms = ln_ref[...]
    table = jnp.zeros((SLOTS, DIM), jnp.float32)
    total = jnp.zeros((SLOTS, 1), jnp.float32)
    for h in range(HEADS):
        grad = g_ref[:, h * DIM : (h + 1) * DIM].astype(jnp.float32)
        wide = o_ref[:, h * DIM : (h + 1) * DIM].astype(jnp.float32)
        low = (gate_col * grad).astype(jnp.bfloat16)
        dout[h] = low
        delta = jnp.sum(low.astype(jnp.float32) * wide, axis=1, keepdims=True)
        total += jnp.sum(grad * wide, axis=1, keepdims=True)
        table = jnp.where(lane == 8 * h, norms[:, h : h + 1] * LOG2E, table)
        table = jnp.where(lane == 8 * h + 1, delta, table)
    table = jnp.where(lane == 8 * HEADS, total, table)
    flat = jnp.concatenate([table, jnp.zeros((64, DIM), jnp.float32)], axis=0).T
    which = lax.broadcasted_iota(jnp.int32, (DIM, 256), 0)
    good = jnp.concatenate(
        [valid.astype(jnp.float32), jnp.zeros((1, 64), jnp.float32)], axis=1
    )
    is_norm = (which % 8 == 0) & (which < 8 * HEADS)
    flat = jnp.where(is_norm & (good < 0.5), FAR, flat)
    stat[...] = flat[: 8 * HEADS + 8]
    rbuf[tp] = stat[pl.ds(8 * HEADS, 8), :]

    pl.semaphore_wait(barrier, SHARDS - 1 + 3)

    def remote(src, dst, ssem, rsem, to):
        return pltpu.make_async_remote_copy(
            src_ref=src, dst_ref=dst, send_sem=ssem, recv_sem=rsem,
            device_id=(to, tp), device_id_type=MESH,
        )

    def push(src, dst, ssem, rsem, to):
        @pl.when(to == me)
        def _():
            pltpu.make_async_copy(src, dst, rsem).start()

        @pl.when(to != me)
        def _():
            remote(src, dst, ssem, rsem, to).start()

    def drain(src, dst, ssem, rsem, to):
        @pl.when(to != me)
        def _():
            remote(src, dst, ssem, rsem, to).wait_send()

    def arrived(dst, rsem):
        remote(dst, dst, dq_ssem.at[0], rsem, (me + 1) % SHARDS).wait_recv()

    def chip_of(role, h):
        a = role * HEADS + h
        cz = a // 3
        return cz * 8 + ((cz + 1 + a % 3) % 4) * 2

    key_role = (me >= CUT).astype(jnp.int32)
    key_slot = me - CUT * key_role
    query_slot = me // 2

    def lanes(ref, h):
        return ref.at[:, pl.ds(pl.multiple_of(h * DIM, DIM), DIM)]

    def key_copies(h, act):
        chip = chip_of(key_role, h)
        for core in range(2):
            act(lanes(k_hbm, h), kbuf.at[key_slot], kv_ssem.at[h, core, 0], kv_rsem.at[key_slot, 0], chip + core)
            act(lanes(v_hbm, h), vbuf.at[key_slot], kv_ssem.at[h, core, 1], kv_rsem.at[key_slot, 1], chip + core)

    def query_copies(h, role, act):
        to = chip_of(role, h) + c
        act(lanes(q_hbm, h), qbuf.at[query_slot], q_ssem.at[h, role, 0], q_rsem.at[query_slot, 0], to)
        act(dout.at[h], gbuf.at[query_slot], q_ssem.at[h, role, 1], q_rsem.at[query_slot, 1], to)
        act(
            stat.at[pl.ds(pl.multiple_of(h * 8, 8), 8), :], sbuf.at[query_slot],
            q_ssem.at[h, role, 2], q_rsem.at[query_slot, 2], to,
        )

    def outgoing(act):
        def keys(h, _):
            key_copies(h, act)
            return 0

        def queries(h, _):
            query_copies(h, 0, act)

            @pl.when(me >= 8)
            def _():
                query_copies(h, 1, act)

            return 0

        lax.fori_loop(0, HEADS, keys, 0)
        lax.fori_loop(0, HEADS, queries, 0)

    outgoing(push)

    def router_copy(i):
        return pltpu.make_async_remote_copy(
            src_ref=stat.at[pl.ds(8 * HEADS, 8), :], dst_ref=rbuf.at[tp],
            send_sem=r_ssem.at[i], recv_sem=r_rsem.at[tp],
            device_id=(me, (tp + i) % 4), device_id_type=MESH,
        )

    for i in range(1, 4):
        router_copy(i).start()

    place = z * 3 + (y - z + 3) % 4
    role = place // HEADS
    head = place % HEADS
    first_key = role * CUT
    n_chunks = jnp.where(role == 0, CUT // 2, REST // 2)

    def chunks_at(b):
        return jnp.where(role == 0, jnp.minimum(4 * b + 4, CUT // 2), jnp.maximum(4 * b - 1, 0))

    def result_copies(kc, act):
        for half in range(2):
            slot = 2 * kc + half
            act(dksend.at[slot], dkrecv.at[head, c], dkv_ssem.at[slot, 0], dkv_rsem.at[head, c, 0], first_key + slot)
            act(dvsend.at[slot], dvrecv.at[head, c], dkv_ssem.at[slot, 1], dkv_rsem.at[head, c, 1], first_key + slot)

    def grad_copy(i, act):
        act(dqsend.at[i], dqrecv.at[head, role], dq_ssem.at[i], dq_rsem.at[head, role], 2 * i + c)

    scale = DIM ** -0.5

    @pl.when(y != z)
    def _():
        def make_ids(i, _):
            shard = first_key + i
            row = lax.broadcasted_iota(jnp.int32, (1, SLOTS), 1) + shard * SLOTS
            row = jnp.where(pos_ref[pl.ds(shard, 1), :] >= 0, row.astype(jnp.float32), NEVER)
            rowid[i] = column(row)
            return 0

        lax.fori_loop(0, 2 * n_chunks, make_ids, 0)

        def clear(i, _):
            dkacc[i] = jnp.zeros((2 * SLOTS, DIM), jnp.float32)
            dvacc[i] = jnp.zeros((2 * SLOTS, DIM), jnp.float32)
            return 0

        lax.fori_loop(0, n_chunks, clear, 0)

        def query_block(b, _):
            def wait_query(i, _):
                arrived(qbuf.at[i], q_rsem.at[i, 0])
                arrived(gbuf.at[i], q_rsem.at[i, 1])
                arrived(sbuf.at[i], q_rsem.at[i, 2])
                return 0

            lax.fori_loop(BLOCK * b, BLOCK * b + BLOCK, wait_query, 0)

            def wait_key(i, _):
                arrived(kbuf.at[i], kv_rsem.at[i, 0])
                arrived(vbuf.at[i], kv_rsem.at[i, 1])
                return 0

            before = jnp.where(b == role, 0, chunks_at(b - 1))
            count = chunks_at(b)
            lax.fori_loop(2 * before, 2 * count, wait_key, 0)

            first = pl.ds(BLOCK * b, BLOCK)
            stats = [sbuf[BLOCK * b + j] for j in range(BLOCK)]
            norm_row = jnp.concatenate([s[0:1, :SLOTS] for s in stats], axis=1)
            delta_row = jnp.concatenate([s[1:2, :SLOTS] for s in stats], axis=1)
            step = lax.broadcasted_iota(jnp.int32, (1, SLOTS), 1)
            col_row = jnp.concatenate(
                [(step + (2 * (BLOCK * b + j) + c) * SLOTS).astype(jnp.float32) for j in range(BLOCK)], axis=1
            )
            dqacc[...] = jnp.zeros_like(dqacc)

            def chunk(kc, _):
                two = pl.ds(2 * kc, 2)
                query = qbuf[first].reshape(BLOCK * SLOTS, DIM)
                grad = gbuf[first].reshape(BLOCK * SLOTS, DIM)
                key = kbuf[two].reshape(2 * SLOTS, DIM)
                value = vbuf[two].reshape(2 * SLOTS, DIM)
                ids = rowid[two].reshape(2 * SLOTS, DIM)
                nt = (((1,), (1,)), ((), ()))
                tn = (((0,), (0,)), ((), ()))
                score = lax.dot_general(key, query, nt, preferred_element_type=jnp.float32)
                score = score * (scale * LOG2E) - norm_row
                ids = jnp.concatenate([ids] * (BLOCK * SLOTS // DIM), axis=1)
                prob = jnp.exp2(jnp.where(ids <= col_row, score, -FAR))
                dprob = lax.dot_general(value, grad, nt, preferred_element_type=jnp.float32)
                dscore = (prob * (dprob - delta_row)).astype(jnp.bfloat16)
                prob_low = prob.astype(jnp.bfloat16)
                dvacc[kc] += jnp.dot(prob_low, grad, preferred_element_type=jnp.float32)
                dkacc[kc] += jnp.dot(dscore, query, preferred_element_type=jnp.float32)
                dqacc[...] += lax.dot_general(key, dscore, tn, preferred_element_type=jnp.float32)

                @pl.when(b == SHARDS // (2 * BLOCK) - 1)
                def _():
                    dksend[two] = (dkacc[kc] * scale).astype(jnp.bfloat16).reshape(2, SLOTS, DIM)
                    dvsend[two] = dvacc[kc].astype(jnp.bfloat16).reshape(2, SLOTS, DIM)
                    result_copies(kc, push)

                return 0

            lax.fori_loop(0, count, chunk, 0)
            dqsend[first] = (dqacc[...].T * scale).astype(jnp.bfloat16).reshape(BLOCK, SLOTS, DIM)

            def give(i, _):
                grad_copy(i, push)
                return 0

            lax.fori_loop(BLOCK * b, BLOCK * b + BLOCK, give, 0)
            return 0

        lax.fori_loop(role, SHARDS // (2 * BLOCK), query_block, 0)

    for i in range(1, 4):
        from_tp = (tp + i) % 4
        arrived(rbuf.at[from_tp], r_rsem.at[from_tp])
    dots = rbuf[0, 0:1, :SLOTS] + rbuf[1, 0:1, :SLOTS] + rbuf[2, 0:1, :SLOTS] + rbuf[3, 0:1, :SLOTS]
    rg_out[...] = jnp.where(valid, gate * (1.0 - gate) * dots, 0.0)

    def add_up(h, _):
        cols = pl.ds(pl.multiple_of(h * DIM, DIM), DIM)
        arrived(dqrecv.at[h, 0], dq_rsem.at[h, 0])

        @pl.when(me >= 8)
        def _():
            arrived(dqrecv.at[h, 1], dq_rsem.at[h, 1])
            both = dqrecv[h, 0].astype(jnp.float32) + dqrecv[h, 1].astype(jnp.float32)
            dq_out[:, cols] = both.astype(jnp.bfloat16)

        @pl.when(me < 8)
        def _():
            dq_out[:, cols] = dqrecv[h, 0]

        for core in range(2):
            arrived(dkrecv.at[h, core], dkv_rsem.at[h, core, 0])
            arrived(dvrecv.at[h, core], dkv_rsem.at[h, core, 1])
        both = dkrecv[h, 0].astype(jnp.float32) + dkrecv[h, 1].astype(jnp.float32)
        dk_out[:, cols] = both.astype(jnp.bfloat16)
        both = dvrecv[h, 0].astype(jnp.float32) + dvrecv[h, 1].astype(jnp.float32)
        dv_out[:, cols] = both.astype(jnp.bfloat16)
        return 0

    lax.fori_loop(0, HEADS, add_up, 0)

    outgoing(drain)
    for i in range(1, 4):
        router_copy(i).wait_send()

    @pl.when(y != z)
    def _():
        def end_results(kc, _):
            result_copies(kc, drain)
            return 0

        def end_grads(i, _):
            grad_copy(i, drain)
            return 0

        lax.fori_loop(0, n_chunks, end_results, 0)
        lax.fori_loop(BLOCK * role, SHARDS // 2, end_grads, 0)


def body(q, k, v, o, g, norm, logit, positions):
    low, wide = jnp.bfloat16, jnp.float32
    whole = pl.BlockSpec(memory_space=pltpu.VMEM)
    far = pl.BlockSpec(memory_space=pl.ANY)
    dma = pltpu.SemaphoreType.DMA
    tile = (SLOTS, DIM)
    out = jax.ShapeDtypeStruct((SLOTS, HEADS * DIM), low)
    dq, dk, dv, router = pl.pallas_call(
        kernel,
        out_shape=(out, out, out, jax.ShapeDtypeStruct((1, SLOTS), wide)),
        in_specs=[far, far, far, whole, whole, whole, whole, whole],
        out_specs=(whole, whole, whole, whole),
        scratch_shapes=[
            pltpu.VMEM((HEADS,) + tile, low),
            pltpu.VMEM((8 * HEADS + 8, 256), wide),
            pltpu.VMEM((4, 8, 256), wide),
            pltpu.VMEM((REST,) + tile, low),
            pltpu.VMEM((REST,) + tile, low),
            pltpu.VMEM((16,) + tile, low),
            pltpu.VMEM((16,) + tile, low),
            pltpu.VMEM((16, 8, 256), wide),
            pltpu.VMEM((REST,) + tile, wide),
            pltpu.VMEM((REST // 2, 2 * SLOTS, DIM), wide),
            pltpu.VMEM((REST // 2, 2 * SLOTS, DIM), wide),
            pltpu.VMEM((DIM, BLOCK * SLOTS), wide),
            pltpu.VMEM((REST,) + tile, low),
            pltpu.VMEM((REST,) + tile, low),
            pltpu.VMEM((16,) + tile, low),
            pltpu.VMEM((HEADS, 2) + tile, low),
            pltpu.VMEM((HEADS, 2) + tile, low),
            pltpu.VMEM((HEADS, 2) + tile, low),
            dma((HEADS, 2, 2)),
            dma((HEADS, 2, 3)),
            dma((REST, 2)),
            dma((16, 3)),
            dma((REST, 2)),
            dma((16,)),
            dma((HEADS, 2, 2)),
            dma((HEADS, 2)),
            dma((4,)),
            dma((4,)),
        ],
        compiler_params=pltpu.CompilerParams(
            collective_id=0, has_side_effects=True, vmem_limit_bytes=56 * 2**20
        ),
        cost_estimate=pl.CostEstimate(flops=9_000_000_000, bytes_accessed=4_000_000, transcendentals=6_000_000),
    )(q, k, v, o, g, norm, logit.reshape(1, SLOTS), positions.reshape(SHARDS, SLOTS))
    return dq, dk, dv, router.reshape(SLOTS)


def solution(mesh):
    split = P("seq", "tp")
    return jax.shard_map(
        body,
        mesh=mesh,
        in_specs=(split, split, split, split, split, split, P("seq"), P()),
        out_specs=(split, split, split, P("seq")),
        check_vma=False,
    )
```

time: 394 us -> 104 us (0.26)
  waiting for transfers between devices: 174 us -> 0 us
  Pallas kernels: 0 us -> 96.5 us
  local copies, waits for them, and re-layouts: 77.7 us -> 6.29 us
  blocking collectives: 54.7 us -> 0 us
  matrix products: 47.9 us -> 0 us
  other arithmetic: 17.6 us -> 0 us
  between operations: 13.8 us -> 0.66 us
  loops' own time: 4.71 us -> 0 us
    reduce_scatter x1 -> x0, waiting for transfers between devices: 119 us -> none  [body(): lax.psum_scatter(terms, 'seq', scatter_dimension=0, tiled=True)]
    pallas_call x0 -> x1, Pallas kernels: none -> 96.5 us  [body(): pl.pallas_call(kernel, out_shape=(out, out, out, jax.ShapeDtypeStruct((1,...]
    all_gather x2 -> x0, waiting for transfers between devices: 54.6 us -> none  [the longest x1 54.6 us: body(): lax.all_gather(dout, 'seq', axis=0, tiled=True)]
    dot_general x30 -> x0, matrix products: 47.9 us -> none  [the longest x6 13.5 us: step(): jnp.einsum('hqk,khd->qhd', dscore, local_key, preferred_element_type=jnp....]
    all_gather x2 -> x0, blocking collectives: 47.2 us -> none  [the longest x1 24.7 us: body(): lax.all_gather(log_norm, 'seq', axis=0, tiled=True)]
    dynamic_slice x24 -> x0, local copies, waits for them, and re-layouts: 42.8 us -> none  [the longest x12 29 us: step(): lax.dynamic_slice_in_dim(dout_all, start, block, 0)]
    dynamic_update_slice x12 -> x0, local copies, waits for them, and re-layouts: 25.5 us -> none  [body(): lax.scan(step, (empty, empty), jnp.arange(steps_count, dtype=jnp.int32))]
    psum x1 -> x0, blocking collectives: 7.48 us -> none  [body(): total_dot = lax.psum(partial_dot, 'tp')]
  transfers between devices with their start and end apart: 3 -> 0, of which waited for: 2 -> 0; matrix products, arithmetic and copies ran while one was open for 2% -> 0% of each run, Pallas kernels for 0% -> 0%
where the time goes in v1:
time: 104 us; the launch traced here: 103 us
  Pallas kernels  96.5 us (93%)
  local copies, waits for them, and re-layouts  6.29 us (6%)
    pallas_call x1, Pallas kernels, body(): pl.pallas_call(kernel, out_shape=(out, out, out, jax.ShapeDtypeStruct((1,...  96.5 us
    unnamed x13, local copies, waits for them, and re-layouts  4.86 us

profile of v1, /device:TPU:102, one launch (start us, length us, event | category | flops | bytes accessed | tf_op | source)
XLA Modules:
  0.0 103.5 jit_solution(4509424281575881207)
XLA Ops:
  0.6 0.0 copy-start.2
  0.6 1.4 %reshape.18.pos_ref = s32[32,192]{1,0:T(8,128)} reshape(s32[6144]{0:T(1024)} %param.15) | data formatting | bytes 49152 | tf_op jit(solution)/shard_map/reshape | solution.py:361
  2.1 0.0 copy-done.2
  2.1 0.8 copy.12.ln_ref
  2.8 96.5 %shard_map.111 = (bf16[192,768]{1,0:T(8,128)(2,1)}, bf16[192,768]{1,0:T(8,128)(2,1)}, bf16[192,768]{1,0:T(8,128)(2,1)}, f32[1,192]{1,0:T(1,128)}) custom-call(bf16[192,768]{1,0:T(8,128)(2,1)} %q_hbm.1, bf16[192,768]{1,0:T(8,128)(2,1)} %k_hbm.1, bf16[192,768]{1,0:T(8,128)(2,1)} %v_hbm.1, bf16[192,768]{1,0:T(8,128)(2,1)} %o_ref.1, bf16[192,768]{1,0:T(8,128)(2,1)} %g_ref.1, ...), custom_call_target="tpu_custom_call" | custom-call | flops 8999999488 | bytes 4000000 | tf_op jit(solution)/shard_map/pallas_call | solution.py:322
  99.4 0.0 copy-start.1
  99.4 1.7 %copy.17 = bf16[192,768]{1,0:T(8,128)(2,1)} copy(bf16[192,768]{1,0:T(8,128)(2,1)} %get-tuple-element.16) | data formatting | bytes 589824
  101.1 0.0 copy-done.1
  101.1 0.0 copy-start
  101.1 0.7 copy.18
  101.8 0.4 copy-done
  102.2 0.0 copy-start.3
  102.2 0.7 copy.19
  102.9 0.0 copy-done.3
  102.9 0.6 copy.20
Async XLA Ops:
  0.6 1.4 %copy-start.2 = (f32[192,6]{0,1:T(8,128)S(1)}, f32[192,6]{0,1:T(8,128)}, u32[]{:S(2)}) copy-start(f32[192,6]{0,1:T(8,128)} %param.13) | copy-start | bytes 13828
  99.4 1.8 %copy-start.1 = (bf16[192,768]{1,0:T(8,128)(2,1)S(1)}, bf16[192,768]{1,0:T(8,128)(2,1)}, u32[]{:S(2)}) copy-start(bf16[192,768]{1,0:T(8,128)(2,1)} %get-tuple-element.17) | copy-start | bytes 884740
  101.1 1.1 %copy-start = (bf16[192,768]{1,0:T(8,128)(2,1)S(1)}, bf16[192,768]{1,0:T(8,128)(2,1)}, u32[]{:S(2)}) copy-start(bf16[192,768]{1,0:T(8,128)(2,1)} %get-tuple-element.18) | copy-start | bytes 884740
  102.2 0.7 copy-start.3

commit v2 on v1

v2 whole, which is shorter than its diff:
```python
import math

import jax
import jax.numpy as jnp
from jax import lax
from jax.experimental import pallas as pl
from jax.experimental.pallas import tpu as pltpu
from jax.sharding import PartitionSpec as P

MESH = pl.DeviceIdType.MESH
LOG2E = math.log2(math.e)
SLOTS = 192
HEADS = 6
DIM = 128
SHARDS = 32
CUT = 12
REST = SHARDS - CUT
BLOCK = 4
FAR = 1e30
NEVER = 1e9


def column(row):
    top = jnp.broadcast_to(row[:, :128], (128, 128)).T
    rest = jnp.concatenate([row[:, 128:], row[:, 128:]], axis=1)
    low = jnp.broadcast_to(rest, (128, 128)).T
    return jnp.concatenate([top, low[:64]], axis=0)


def kernel(
    q_hbm, k_hbm, v_hbm, o_ref, g_ref, ln_ref, logit_ref, pos_ref,
    dqa_out, dqb_out, dk_out, dv_out, rg_out,
    dout, stat, rbuf, kbuf, vbuf, qbuf, gbuf, sbuf, rowid, dkacc, dvacc, dqacc,
    xsend, xrecv, dkvsend, dqsend,
    kv_ssem, q_ssem, kv_rsem, q_rsem, fwd_ssem, x_ssem, x_rsem, dkv_ssem, dq_ssem, dkv_rsem, dq_rsem, r_ssem, r_rsem,
):
    me = lax.axis_index("seq")
    tp = lax.axis_index("tp")
    z, y, c = me // 8, (me // 2) % 4, me % 2
    sibling = me + 1 - 2 * c

    barrier = pltpu.get_barrier_semaphore()

    def greet(i, _):
        pl.semaphore_signal(barrier, inc=1, device_id=((me + i) % SHARDS, tp), device_id_type=MESH)
        return 0

    lax.fori_loop(1, SHARDS, greet, 0)
    for i in range(1, 4):
        pl.semaphore_signal(barrier, inc=1, device_id=(me, (tp + i) % 4), device_id_type=MESH)

    logit = logit_ref[...]
    gate = 1.0 / (1.0 + jnp.exp(-logit))
    at = (me * 3) // 2
    top, low = pos_ref[pl.ds(at, 1), :], pos_ref[pl.ds(at + 1, 1), :]
    even = jnp.concatenate([top, low[:, :64]], axis=1)
    odd = jnp.concatenate([top[:, 64:], low], axis=1)
    valid = jnp.where(c == 0, even, odd) >= 0
    gate_col = column(gate)
    lane = lax.broadcasted_iota(jnp.int32, (SLOTS, DIM), 1)
    table = jnp.zeros((SLOTS, DIM), jnp.float32)
    total = jnp.zeros((SLOTS, 1), jnp.float32)
    for h in range(HEADS):
        grad = g_ref[:, h * DIM : (h + 1) * DIM].astype(jnp.float32)
        wide = o_ref[:, h * DIM : (h + 1) * DIM].astype(jnp.float32)
        low = (gate_col * grad).astype(jnp.bfloat16)
        dout[h] = low
        delta = jnp.sum(low.astype(jnp.float32) * wide, axis=1, keepdims=True)
        total += jnp.sum(grad * wide, axis=1, keepdims=True)
        table = jnp.where(lane == 8 * h + 1, delta, table)
    table = jnp.where(lane == 8 * HEADS, total, table)
    flat = jnp.concatenate([table, jnp.zeros((64, DIM), jnp.float32)], axis=0).T
    stat[...] = flat[: 8 * HEADS + 8]
    for h in range(HEADS):
        norm = jnp.where(valid, ln_ref[h : h + 1, :] * LOG2E, FAR)
        stat[8 * h : 8 * h + 1, :SLOTS] = norm
    rbuf[tp] = stat[pl.ds(8 * HEADS, 8), :]

    place = z * 3 + (y - z + 3) % 4
    role = place // HEADS
    head = place % HEADS
    first_key = role * CUT
    n_chunks = jnp.where(role == 0, CUT // 2, REST // 2)

    def chunks_at(b):
        return jnp.where(role == 0, jnp.minimum(4 * b + 4, CUT // 2), jnp.maximum(4 * b - 2, 0))

    @pl.when(y != z)
    def _():
        def make_ids(i, _):
            for j in range(3):
                at = (first_key * 3) // 2 + 3 * i + j
                row = lax.broadcasted_iota(jnp.int32, (1, DIM), 1) + at * DIM
                row = jnp.where(pos_ref[pl.ds(at, 1), :] >= 0, row.astype(jnp.float32), NEVER)
                rowid[i, DIM * j : DIM * (j + 1), :] = jnp.broadcast_to(row, (DIM, DIM)).T
            dkacc[i] = jnp.zeros((2 * SLOTS, DIM), jnp.float32)
            dvacc[i] = jnp.zeros((2 * SLOTS, DIM), jnp.float32)
            return 0

        lax.fori_loop(0, n_chunks, make_ids, 0)

        @pl.when(role == 1)
        def _():
            for i in (CUT // 2 - 2, CUT // 2 - 1):
                qbuf[i] = jnp.zeros((SLOTS, DIM), jnp.bfloat16)
                gbuf[i] = jnp.zeros((SLOTS, DIM), jnp.bfloat16)
                sbuf[i] = jnp.zeros((8, 256), jnp.float32)

    pl.semaphore_wait(barrier, SHARDS - 1 + 3)

    def remote(src, dst, ssem, rsem, to):
        return pltpu.make_async_remote_copy(
            src_ref=src, dst_ref=dst, send_sem=ssem, recv_sem=rsem,
            device_id=(to, tp), device_id_type=MESH,
        )

    def push(src, dst, ssem, rsem, to):
        @pl.when(to == me)
        def _():
            pltpu.make_async_copy(src, dst, rsem).start()

        @pl.when(to != me)
        def _():
            remote(src, dst, ssem, rsem, to).start()

    def drain(src, dst, ssem, rsem, to):
        @pl.when(to != me)
        def _():
            remote(src, dst, ssem, rsem, to).wait_send()

    def arrived(dst, rsem):
        remote(dst, dst, dq_ssem.at[0], rsem, (me + 1) % SHARDS).wait_recv()

    def chip_of(role, h):
        a = role * HEADS + h
        cz = a // 3
        return cz * 8 + ((cz + 1 + a % 3) % 4) * 2

    key_role = (me >= CUT).astype(jnp.int32)
    key_slot = me - CUT * key_role
    query_slot = me // 2

    def lanes(ref, h):
        return ref.at[:, pl.ds(pl.multiple_of(h * DIM, DIM), DIM)]

    def key_copies(h, act):
        to = chip_of(key_role, h) + c
        act(lanes(k_hbm, h), kbuf.at[key_slot], kv_ssem.at[h, 0], kv_rsem.at[key_slot, 0], to)
        act(lanes(v_hbm, h), vbuf.at[key_slot], kv_ssem.at[h, 1], kv_rsem.at[key_slot, 1], to)

    def query_copies(h, role, act):
        to = chip_of(role, h) + c
        act(lanes(q_hbm, h), qbuf.at[query_slot], q_ssem.at[h, role, 0], q_rsem.at[query_slot, 0], to)
        act(dout.at[h], gbuf.at[query_slot], q_ssem.at[h, role, 1], q_rsem.at[query_slot, 1], to)
        act(
            stat.at[pl.ds(pl.multiple_of(h * 8, 8), 8), :], sbuf.at[query_slot],
            q_ssem.at[h, role, 2], q_rsem.at[query_slot, 2], to,
        )

    def outgoing(act):
        chip = me // 2

        def keys(i, _):
            key_copies((chip + i) % HEADS, act)
            return 0

        def queries(i, _):
            target = ((chip * 3) // 4 + i) % (2 * HEADS)

            @pl.when((target < HEADS) | (me >= CUT))
            def _():
                query_copies(target % HEADS, target // HEADS, act)

            return 0

        lax.fori_loop(0, HEADS, keys, 0)
        lax.fori_loop(0, 2 * HEADS, queries, 0)

    outgoing(push)

    def router_copy(i):
        return pltpu.make_async_remote_copy(
            src_ref=stat.at[pl.ds(8 * HEADS, 8), :], dst_ref=rbuf.at[tp],
            send_sem=r_ssem.at[i], recv_sem=r_rsem.at[tp],
            device_id=(me, (tp + i) % 4), device_id_type=MESH,
        )

    for i in range(1, 4):
        router_copy(i).start()

    def forward_copies(kc, act):
        slot = 2 * kc + c
        act(kbuf.at[slot], kbuf.at[slot], fwd_ssem.at[kc, 0], kv_rsem.at[slot, 0], sibling)
        act(vbuf.at[slot], vbuf.at[slot], fwd_ssem.at[kc, 1], kv_rsem.at[slot, 1], sibling)

    def exchange_copy(kc, act):
        act(xsend.at[kc], xrecv.at[kc], x_ssem.at[kc], x_rsem.at[kc], sibling)

    def result_copies(kc, act):
        owner = first_key + 2 * kc + c
        act(dkvsend.at[kc, 0], lanes(dk_out, head), dkv_ssem.at[kc, 0], dkv_rsem.at[head, 0], owner)
        act(dkvsend.at[kc, 1], lanes(dv_out, head), dkv_ssem.at[kc, 1], dkv_rsem.at[head, 1], owner)

    def grad_copy(i, act):
        @pl.when(role == 0)
        def _():
            act(dqsend.at[i], lanes(dqa_out, head), dq_ssem.at[i], dq_rsem.at[head, 0], 2 * i + c)

        @pl.when(role == 1)
        def _():
            act(dqsend.at[i], lanes(dqb_out, head), dq_ssem.at[i], dq_rsem.at[head, 1], 2 * i + c)

    scale = DIM ** -0.5
    last = SHARDS // (2 * BLOCK) - 1
    first_query = role * (CUT // 2)

    @pl.when(y != z)
    def _():
        def query_block(b, _):
            def wait_query(i, _):
                arrived(qbuf.at[i], q_rsem.at[i, 0])
                arrived(gbuf.at[i], q_rsem.at[i, 1])
                arrived(sbuf.at[i], q_rsem.at[i, 2])
                return 0

            def own_key(kc, _):
                slot = 2 * kc + c
                arrived(kbuf.at[slot], kv_rsem.at[slot, 0])
                arrived(vbuf.at[slot], kv_rsem.at[slot, 1])
                forward_copies(kc, push)
                return 0

            def other_key(kc, _):
                slot = 2 * kc + 1 - c
                arrived(kbuf.at[slot], kv_rsem.at[slot, 0])
                arrived(vbuf.at[slot], kv_rsem.at[slot, 1])
                return 0

            before = jnp.where(b == role, 0, chunks_at(b - 1))
            count = chunks_at(b)
            start = jnp.maximum(BLOCK * b, first_query)
            lax.fori_loop(before, count, own_key, 0)
            lax.fori_loop(start, BLOCK * b + BLOCK, wait_query, 0)
            lax.fori_loop(before, count, other_key, 0)

            first = pl.ds(BLOCK * b, BLOCK)
            stats = [sbuf[BLOCK * b + j] for j in range(BLOCK)]
            norm_row = jnp.concatenate([s[0:1, :SLOTS] for s in stats], axis=1)
            delta_row = jnp.concatenate([s[1:2, :SLOTS] for s in stats], axis=1)
            step = lax.broadcasted_iota(jnp.int32, (1, SLOTS), 1)
            col_row = jnp.concatenate(
                [(step + (2 * (BLOCK * b + j) + c) * SLOTS).astype(jnp.float32) for j in range(BLOCK)], axis=1
            )
            dqacc[...] = jnp.zeros_like(dqacc)

            def turn(i):
                return (i + (head * count) // HEADS) % count

            def finish(kc):
                mine = pl.ds(pl.multiple_of(c * SLOTS, SLOTS), SLOTS)
                arrived(xrecv.at[kc], x_rsem.at[kc])
                both = dkacc[kc, mine, :] * scale + xrecv[kc, 0].astype(jnp.float32)
                dkvsend[kc, 0] = both.astype(jnp.bfloat16)
                both = dvacc[kc, mine, :] + xrecv[kc, 1].astype(jnp.float32)
                dkvsend[kc, 1] = both.astype(jnp.bfloat16)
                result_copies(kc, push)

            def chunk(i, _):
                kc = turn(i)
                two = pl.ds(2 * kc, 2)
                query = qbuf[first].reshape(BLOCK * SLOTS, DIM)
                grad = gbuf[first].reshape(BLOCK * SLOTS, DIM)
                key = kbuf[two].reshape(2 * SLOTS, DIM)
                value = vbuf[two].reshape(2 * SLOTS, DIM)
                ids = rowid[kc]
                nt = (((1,), (1,)), ((), ()))
                tn = (((0,), (0,)), ((), ()))
                score = lax.dot_general(key, query, nt, preferred_element_type=jnp.float32)
                score = score * (scale * LOG2E) - norm_row
                ids = jnp.concatenate([ids] * (BLOCK * SLOTS // DIM), axis=1)
                prob = jnp.exp2(jnp.where(ids <= col_row, score, -FAR))
                dprob = lax.dot_general(value, grad, nt, preferred_element_type=jnp.float32)
                dscore = (prob * (dprob - delta_row)).astype(jnp.bfloat16)
                prob_low = prob.astype(jnp.bfloat16)
                dvacc[kc] += jnp.dot(prob_low, grad, preferred_element_type=jnp.float32)
                dkacc[kc] += jnp.dot(dscore, query, preferred_element_type=jnp.float32)
                dqacc[...] += lax.dot_general(key, dscore, tn, preferred_element_type=jnp.float32)

                @pl.when(b == last)
                def _():
                    theirs = pl.ds(pl.multiple_of((1 - c) * SLOTS, SLOTS), SLOTS)
                    xsend[kc, 0] = (dkacc[kc, theirs, :] * scale).astype(jnp.bfloat16)
                    xsend[kc, 1] = dvacc[kc, theirs, :].astype(jnp.bfloat16)
                    exchange_copy(kc, push)

                    @pl.when(i > 0)
                    def _():
                        finish(turn(i - 1))

                return 0

            lax.fori_loop(0, count, chunk, 0)

            @pl.when(b == last)
            def _():
                finish(turn(count - 1))

            dqsend[first] = (dqacc[...].T * scale).astype(jnp.bfloat16).reshape(BLOCK, SLOTS, DIM)

            def give(i, _):
                grad_copy(i, push)
                return 0

            lax.fori_loop(start, BLOCK * b + BLOCK, give, 0)
            return 0

        lax.fori_loop(role, last + 1, query_block, 0)

    for i in range(1, 4):
        from_tp = (tp + i) % 4
        arrived(rbuf.at[from_tp], r_rsem.at[from_tp])
    dots = rbuf[0, 0:1, :SLOTS] + rbuf[1, 0:1, :SLOTS] + rbuf[2, 0:1, :SLOTS] + rbuf[3, 0:1, :SLOTS]
    rg_out[...] = jnp.where(valid, gate * (1.0 - gate) * dots, 0.0)

    def collect(h, _):
        arrived(lanes(dqa_out, h), dq_rsem.at[h, 0])

        @pl.when(me >= CUT)
        def _():
            arrived(lanes(dqb_out, h), dq_rsem.at[h, 1])

        arrived(lanes(dk_out, h), dkv_rsem.at[h, 0])
        arrived(lanes(dv_out, h), dkv_rsem.at[h, 1])
        return 0

    lax.fori_loop(0, HEADS, collect, 0)

    outgoing(drain)
    for i in range(1, 4):
        router_copy(i).wait_send()

    @pl.when(y != z)
    def _():
        def end_results(kc, _):
            forward_copies(kc, drain)
            exchange_copy(kc, drain)
            result_copies(kc, drain)
            return 0

        def end_grads(i, _):
            grad_copy(i, drain)
            return 0

        lax.fori_loop(0, n_chunks, end_results, 0)
        lax.fori_loop(first_query, SHARDS // 2, end_grads, 0)


def finish_kernel(dqa, dqb, dk, dv, router, dq_out, dk_out, dv_out, rg_out, buf, in_sems, out_sems):
    me = lax.axis_index("seq")
    parts = [pltpu.make_async_copy(ref, buf.at[i], in_sems.at[i]) for i, ref in enumerate((dk, dv, dqa, dqb))]
    results = [
        pltpu.make_async_copy(buf.at[i], ref, out_sems.at[i]) for i, ref in enumerate((dk_out, dv_out, dq_out))
    ]
    for i in range(3):
        parts[i].start()

    @pl.when(me >= CUT)
    def _():
        parts[3].start()

    rg_out[...] = router[...]
    for i in range(2):
        parts[i].wait()
        results[i].start()
    parts[2].wait()

    @pl.when(me >= CUT)
    def _():
        parts[3].wait()
        buf[2] = (buf[2].astype(jnp.float32) + buf[3].astype(jnp.float32)).astype(jnp.bfloat16)

    results[2].start()
    for result in results:
        result.wait()


def body(q, k, v, o, g, norm, logit, positions):
    low, wide = jnp.bfloat16, jnp.float32
    whole = pl.BlockSpec(memory_space=pltpu.VMEM)
    far = pl.BlockSpec(memory_space=pl.ANY)
    dma = pltpu.SemaphoreType.DMA
    tile = (SLOTS, DIM)
    half = REST // 2
    out = jax.ShapeDtypeStruct((SLOTS, HEADS * DIM), low)
    row = jax.ShapeDtypeStruct((1, SLOTS), wide)
    dqa, dqb, dk, dv, router = pl.pallas_call(
        kernel,
        out_shape=(out, out, out, out, row),
        in_specs=[far, far, far, whole, whole, whole, whole, whole],
        out_specs=(far, far, far, far, whole),
        scratch_shapes=[
            pltpu.VMEM((HEADS,) + tile, low),
            pltpu.VMEM((8 * HEADS + 8, 256), wide),
            pltpu.VMEM((4, 8, 256), wide),
            pltpu.VMEM((REST,) + tile, low),
            pltpu.VMEM((REST,) + tile, low),
            pltpu.VMEM((16,) + tile, low),
            pltpu.VMEM((16,) + tile, low),
            pltpu.VMEM((16, 8, 256), wide),
            pltpu.VMEM((half, 2 * SLOTS, DIM), wide),
            pltpu.VMEM((half, 2 * SLOTS, DIM), wide),
            pltpu.VMEM((half, 2 * SLOTS, DIM), wide),
            pltpu.VMEM((DIM, BLOCK * SLOTS), wide),
            pltpu.VMEM((half, 2) + tile, low),
            pltpu.VMEM((half, 2) + tile, low),
            pltpu.VMEM((half, 2) + tile, low),
            pltpu.VMEM((16,) + tile, low),
            dma((HEADS, 2)),
            dma((HEADS, 2, 3)),
            dma((REST, 2)),
            dma((16, 3)),
            dma((half, 2)),
            dma((half,)),
            dma((half,)),
            dma((half, 2)),
            dma((16,)),
            dma((HEADS, 2)),
            dma((HEADS, 2)),
            dma((4,)),
            dma((4,)),
        ],
        compiler_params=pltpu.CompilerParams(
            collective_id=0, has_side_effects=True, vmem_limit_bytes=56 * 2**20
        ),
        cost_estimate=pl.CostEstimate(flops=9_000_000_000, bytes_accessed=4_000_000, transcendentals=6_000_000),
    )(q, k, v, o, g, norm.T, logit.reshape(1, SLOTS), positions.reshape(-1, DIM))
    dq, dk, dv, router = pl.pallas_call(
        finish_kernel,
        out_shape=(out, out, out, row),
        in_specs=[far, far, far, far, whole],
        out_specs=(far, far, far, whole),
        scratch_shapes=[
            pltpu.VMEM((4, SLOTS, HEADS * DIM), low),
            dma((4,)),
            dma((3,)),
        ],
        compiler_params=pltpu.CompilerParams(vmem_limit_bytes=56 * 2**20),
    )(dqa, dqb, dk, dv, router)
    return dq, dk, dv, router.reshape(SLOTS)


def solution(mesh):
    split = P("seq", "tp")
    return jax.shard_map(
        body,
        mesh=mesh,
        in_specs=(split, split, split, split, split, split, P("seq"), P()),
        out_specs=(split, split, split, P("seq")),
        check_vma=False,
    )
```

time: 104 us -> 71.3 us (0.69)
  the two profiles are of different devices: /device:TPU:102 before, /device:TPU:62 now
where the time goes in v2:
time: 71.3 us; the launch traced here: 71.2 us
  Pallas kernels  70.5 us (99%)
    pallas_call x1, Pallas kernels, body(): pl.pallas_call(kernel, out_shape=(out, out, out, out, row), in_specs=[far...  67.3 us
    pallas_call x1, Pallas kernels, body(): pl.pallas_call(finish_kernel, out_shape=(out, out, out, row), in_specs=[f...  3.26 us

profile of v2, /device:TPU:62, one launch (start us, length us, event | category | flops | bytes accessed | tf_op | source)
XLA Modules:
  0.0 71.2 jit_solution(2237001875568539299)
XLA Ops:
  0.6 67.3 %shard_map.111 = (bf16[192,768]{1,0:T(8,128)(2,1)}, bf16[192,768]{1,0:T(8,128)(2,1)}, bf16[192,768]{1,0:T(8,128)(2,1)}, bf16[192,768]{1,0:T(8,128)(2,1)}, f32[1,192]{1,0:T(1,128)}) custom-call(bf16[192,768]{1,0:T(8,128)(2,1)} %q_hbm.1, bf16[192,768]{1,0:T(8,128)(2,1)} %k_hbm.1, bf16[192,768]{1,0:T(8,128)(2,1)} %v_hbm.1, bf16[192,768]{1,0:T(8,128)(2,1)} %o_ref.1, ...), custom_call_target="tpu_custom_call" | custom-call | flops 8999999488 | bytes 4000000 | tf_op jit(solution)/shard_map/pallas_call | solution.py:396
  67.9 3.3 %shard_map.112 = (bf16[192,768]{1,0:T(8,128)(2,1)}, bf16[192,768]{1,0:T(8,128)(2,1)}, bf16[192,768]{1,0:T(8,128)(2,1)}, f32[1,192]{1,0:T(1,128)}) custom-call(bf16[192,768]{1,0:T(8,128)(2,1)} %get-tuple-element.13.dqa, bf16[192,768]{1,0:T(8,128)(2,1)} %get-tuple-element.14.dqb, bf16[192,768]{1,0:T(8,128)(2,1)} %get-tuple-element.15.dk, ...), custom_call_target="tpu_custom_call" | custom-call | tf_op jit(solution)/shard_map/pallas_call | solution.py:437

commit v3 on v2

--- a/solution.py
+++ b/solution.py
@@ -216,6 +216,15 @@
 
     @pl.when(y != z)
     def _():
+        def own_key(kc, _):
+            slot = 2 * kc + c
+            arrived(kbuf.at[slot], kv_rsem.at[slot, 0])
+            arrived(vbuf.at[slot], kv_rsem.at[slot, 1])
+            forward_copies(kc, push)
+            return 0
+
+        lax.fori_loop(0, n_chunks, own_key, 0)
+
         def query_block(b, _):
             def wait_query(i, _):
                 arrived(qbuf.at[i], q_rsem.at[i, 0])
@@ -223,13 +232,6 @@
                 arrived(sbuf.at[i], q_rsem.at[i, 2])
                 return 0
 
-            def own_key(kc, _):
-                slot = 2 * kc + c
-                arrived(kbuf.at[slot], kv_rsem.at[slot, 0])
-                arrived(vbuf.at[slot], kv_rsem.at[slot, 1])
-                forward_copies(kc, push)
-                return 0
-
             def other_key(kc, _):
                 slot = 2 * kc + 1 - c
                 arrived(kbuf.at[slot], kv_rsem.at[slot, 0])
@@ -239,7 +241,6 @@
             before = jnp.where(b == role, 0, chunks_at(b - 1))
             count = chunks_at(b)
             start = jnp.maximum(BLOCK * b, first_query)
-            lax.fori_loop(before, count, own_key, 0)
             lax.fori_loop(start, BLOCK * b + BLOCK, wait_query, 0)
             lax.fori_loop(before, count, other_key, 0)
 
@@ -307,11 +308,13 @@
 
             dqsend[first] = (dqacc[...].T * scale).astype(jnp.bfloat16).reshape(BLOCK, SLOTS, DIM)
 
+            n_grads = BLOCK * b + BLOCK - start
+
             def give(i, _):
-                grad_copy(i, push)
+                grad_copy(start + (i + head + 2 * role) % n_grads, push)
                 return 0
 
-            lax.fori_loop(start, BLOCK * b + BLOCK, give, 0)
+            lax.fori_loop(0, n_grads, give, 0)
             return 0
 
         lax.fori_loop(role, last + 1, query_block, 0)

time: 71.3 us -> 69.4 us (0.973)
  the two profiles are of different devices: /device:TPU:62 before, /device:TPU:102 now
where the time goes in v3:
time: 69.4 us; the launch traced here: 69 us
  Pallas kernels  68.4 us (99%)
    pallas_call x1, Pallas kernels, body(): pl.pallas_call(kernel, out_shape=(out, out, out, out, row), in_specs=[far...  65.1 us
    pallas_call x1, Pallas kernels, body(): pl.pallas_call(finish_kernel, out_shape=(out, out, out, row), in_specs=[f...  3.26 us

profile of v3, /device:TPU:102, one launch (start us, length us, event | category | flops | bytes accessed | tf_op | source)
XLA Modules:
  0.0 69.0 jit_solution(7074116145408589793)
XLA Ops:
  0.6 65.1 %shard_map.111 = (bf16[192,768]{1,0:T(8,128)(2,1)}, bf16[192,768]{1,0:T(8,128)(2,1)}, bf16[192,768]{1,0:T(8,128)(2,1)}, bf16[192,768]{1,0:T(8,128)(2,1)}, f32[1,192]{1,0:T(1,128)}) custom-call(bf16[192,768]{1,0:T(8,128)(2,1)} %q_hbm.1, bf16[192,768]{1,0:T(8,128)(2,1)} %k_hbm.1, bf16[192,768]{1,0:T(8,128)(2,1)} %v_hbm.1, bf16[192,768]{1,0:T(8,128)(2,1)} %o_ref.1, ...), custom_call_target="tpu_custom_call" | custom-call | flops 8999999488 | bytes 4000000 | tf_op jit(solution)/shard_map/pallas_call | solution.py:399
  65.8 3.3 %shard_map.112 = (bf16[192,768]{1,0:T(8,128)(2,1)}, bf16[192,768]{1,0:T(8,128)(2,1)}, bf16[192,768]{1,0:T(8,128)(2,1)}, f32[1,192]{1,0:T(1,128)}) custom-call(bf16[192,768]{1,0:T(8,128)(2,1)} %get-tuple-element.13.dqa, bf16[192,768]{1,0:T(8,128)(2,1)} %get-tuple-element.14.dqb, bf16[192,768]{1,0:T(8,128)(2,1)} %get-tuple-element.15.dk, ...), custom_call_target="tpu_custom_call" | custom-call | tf_op jit(solution)/shard_map/pallas_call | solution.py:440

commit v4 on v3

--- a/solution.py
+++ b/solution.py
@@ -28,9 +28,9 @@
 
 
 def kernel(
-    q_hbm, k_hbm, v_hbm, o_ref, g_ref, ln_ref, logit_ref, pos_ref,
+    q_ref, k_hbm, v_hbm, o_ref, g_ref, ln_ref, logit_ref, pos_ref,
     dqa_out, dqb_out, dk_out, dv_out, rg_out,
-    dout, stat, rbuf, kbuf, vbuf, qbuf, gbuf, sbuf, rowid, dkacc, dvacc, dqacc,
+    dout, stat, rbuf, kbuf, vbuf, qbuf, sbuf, rowid, dkacc, dvacc, dqacc,
     xsend, xrecv, dkvsend, dqsend,
     kv_ssem, q_ssem, kv_rsem, q_rsem, fwd_ssem, x_ssem, x_rsem, dkv_ssem, dq_ssem, dkv_rsem, dq_rsem, r_ssem, r_rsem,
 ):
@@ -64,7 +64,8 @@
         grad = g_ref[:, h * DIM : (h + 1) * DIM].astype(jnp.float32)
         wide = o_ref[:, h * DIM : (h + 1) * DIM].astype(jnp.float32)
         low = (gate_col * grad).astype(jnp.bfloat16)
-        dout[h] = low
+        dout[h, 0] = q_ref[:, h * DIM : (h + 1) * DIM]
+        dout[h, 1] = low
         delta = jnp.sum(low.astype(jnp.float32) * wide, axis=1, keepdims=True)
         total += jnp.sum(grad * wide, axis=1, keepdims=True)
         table = jnp.where(lane == 8 * h + 1, delta, table)
@@ -102,8 +103,7 @@
         @pl.when(role == 1)
         def _():
             for i in (CUT // 2 - 2, CUT // 2 - 1):
-                qbuf[i] = jnp.zeros((SLOTS, DIM), jnp.bfloat16)
-                gbuf[i] = jnp.zeros((SLOTS, DIM), jnp.bfloat16)
+                qbuf[i] = jnp.zeros((2, SLOTS, DIM), jnp.bfloat16)
                 sbuf[i] = jnp.zeros((8, 256), jnp.float32)
 
     pl.semaphore_wait(barrier, SHARDS - 1 + 3)
@@ -150,8 +150,7 @@
 
     def query_copies(h, role, act):
         to = chip_of(role, h) + c
-        act(lanes(q_hbm, h), qbuf.at[query_slot], q_ssem.at[h, role, 0], q_rsem.at[query_slot, 0], to)
-        act(dout.at[h], gbuf.at[query_slot], q_ssem.at[h, role, 1], q_rsem.at[query_slot, 1], to)
+        act(dout.at[h], qbuf.at[query_slot], q_ssem.at[h, role, 1], q_rsem.at[query_slot, 1], to)
         act(
             stat.at[pl.ds(pl.multiple_of(h * 8, 8), 8), :], sbuf.at[query_slot],
             q_ssem.at[h, role, 2], q_rsem.at[query_slot, 2], to,
@@ -227,8 +226,7 @@
 
         def query_block(b, _):
             def wait_query(i, _):
-                arrived(qbuf.at[i], q_rsem.at[i, 0])
-                arrived(gbuf.at[i], q_rsem.at[i, 1])
+                arrived(qbuf.at[i], q_rsem.at[i, 1])
                 arrived(sbuf.at[i], q_rsem.at[i, 2])
                 return 0
 
@@ -269,8 +267,8 @@
             def chunk(i, _):
                 kc = turn(i)
                 two = pl.ds(2 * kc, 2)
-                query = qbuf[first].reshape(BLOCK * SLOTS, DIM)
-                grad = gbuf[first].reshape(BLOCK * SLOTS, DIM)
+                query = qbuf[first, 0].reshape(BLOCK * SLOTS, DIM)
+                grad = qbuf[first, 1].reshape(BLOCK * SLOTS, DIM)
                 key = kbuf[two].reshape(2 * SLOTS, DIM)
                 value = vbuf[two].reshape(2 * SLOTS, DIM)
                 ids = rowid[kc]
@@ -399,16 +397,15 @@
     dqa, dqb, dk, dv, router = pl.pallas_call(
         kernel,
         out_shape=(out, out, out, out, row),
-        in_specs=[far, far, far, whole, whole, whole, whole, whole],
+        in_specs=[whole, far, far, whole, whole, whole, whole, whole],
         out_specs=(far, far, far, far, whole),
         scratch_shapes=[
-            pltpu.VMEM((HEADS,) + tile, low),
+            pltpu.VMEM((HEADS, 2) + tile, low),
             pltpu.VMEM((8 * HEADS + 8, 256), wide),
             pltpu.VMEM((4, 8, 256), wide),
             pltpu.VMEM((REST,) + tile, low),
             pltpu.VMEM((REST,) + tile, low),
-            pltpu.VMEM((16,) + tile, low),
-            pltpu.VMEM((16,) + tile, low),
+            pltpu.VMEM((16, 2) + tile, low),
             pltpu.VMEM((16, 8, 256), wide),
             pltpu.VMEM((half, 2 * SLOTS, DIM), wide),
             pltpu.VMEM((half, 2 * SLOTS, DIM), wide),

time: 69.4 us -> 69.5 us (level)
  no operation moved by 1% of the time
where the time goes in v4:
time: 69.5 us; the launch traced here: 69.1 us
  Pallas kernels  68.4 us (98%)
    pallas_call x1, Pallas kernels, body(): pl.pallas_call(kernel, out_shape=(out, out, out, out, row), in_specs=[who...  65.2 us
    pallas_call x1, Pallas kernels, body(): pl.pallas_call(finish_kernel, out_shape=(out, out, out, row), in_specs=[f...  3.26 us

profile of v4, /device:TPU:102, one launch (start us, length us, event | category | flops | bytes accessed | tf_op | source)
XLA Modules:
  0.0 69.1 jit_solution(13556078211883024073)
XLA Ops:
  0.6 65.2 %shard_map.111 = (bf16[192,768]{1,0:T(8,128)(2,1)}, bf16[192,768]{1,0:T(8,128)(2,1)}, bf16[192,768]{1,0:T(8,128)(2,1)}, bf16[192,768]{1,0:T(8,128)(2,1)}, f32[1,192]{1,0:T(1,128)}) custom-call(bf16[192,768]{1,0:T(8,128)(2,1)} %q_ref.1, bf16[192,768]{1,0:T(8,128)(2,1)} %k_hbm.1, bf16[192,768]{1,0:T(8,128)(2,1)} %v_hbm.1, bf16[192,768]{1,0:T(8,128)(2,1)} %o_ref.1, ...), custom_call_target="tpu_custom_call" | custom-call | flops 8999999488 | bytes 4000000 | tf_op jit(solution)/shard_map/pallas_call | solution.py:397
  65.8 3.3 %shard_map.112 = (bf16[192,768]{1,0:T(8,128)(2,1)}, bf16[192,768]{1,0:T(8,128)(2,1)}, bf16[192,768]{1,0:T(8,128)(2,1)}, f32[1,192]{1,0:T(1,128)}) custom-call(bf16[192,768]{1,0:T(8,128)(2,1)} %get-tuple-element.13.dqa, bf16[192,768]{1,0:T(8,128)(2,1)} %get-tuple-element.14.dqb, bf16[192,768]{1,0:T(8,128)(2,1)} %get-tuple-element.15.dk, ...), custom_call_target="tpu_custom_call" | custom-call | tf_op jit(solution)/shard_map/pallas_call | solution.py:437
